TPU v7x, 256 devices: a whole 4x4x8 slice. The times are simulated.
256 devices in a mesh: fsdp: 64 (over y, x_hi, z), tensor: 4 (over x_lo, core).
Axes of the slice: x: 4 (x_hi: 2, x_lo: 2; x = x_hi * 2 + x_lo), y: 4, z: 8, core: 2. Of those that a mesh axis runs over, the one named last changes fastest.
Arguments:
- activations: bfloat16 [98304, 5120], P('fsdp', 'tensor'), may hold values from -6 to 6
- key_weight: bfloat16 [5120, 1024], P('tensor'), may hold values from -0.078125 to 0.078125
- key_gain: float32 [128], replicated, may hold values from 0.1 to 1.9
- span_start: int32 [64], P('fsdp'), may hold values from 0 to 4095
- next_weight: bfloat16 [2, 5120, 1024], P(None, ('fsdp', 'tensor')), may hold values from -16 to 16
Outputs:
- new_keys: bfloat16 [98304, 1024], P('fsdp', 'tensor')
- next_scaled: bfloat16 [2, 5120, 1024], P(None, None, 'tensor')
- block_max: float32 [2, 40, 8], P(None, None, 'tensor')
All inputs are finite; a program needn't handle non-finite values. Where the computation divides by a largest or mean magnitude, that divisor is 1e-20 or more.
Results may differ from a plain program's by a relative error of at most 0.015.
Values may be sent and summed in bfloat16 or wider, within the bound.
No kernel may reach another device: no remote copies, remote signals or barrier semaphores. Data moves between devices by JAX's collectives and lax.ppermute only.
A program may use at most 128 MiB of HBM per device.

v0:
```python
import math

import jax
import jax.numpy as jnp
from jax import lax
from jax.sharding import PartitionSpec as P

BLOCK = 128


def finish_keys(running, span_begin, key_gain):
    token_count = running.shape[0]
    head_size = key_gain.shape[0]
    half_size = head_size // 2
    head_view = running.reshape(token_count, -1, head_size)
    normed = (
        head_view
        * lax.rsqrt(jnp.mean(head_view * head_view, axis=-1, keepdims=True) + 1e-06)
        * key_gain
    )
    positions = (span_begin + jnp.arange(token_count, dtype=jnp.int32)).astype(jnp.float32)
    frequency = jnp.exp(
        jnp.arange(half_size, dtype=jnp.float32) * (-2.0 * math.log(1000000.0) / head_size)
    )
    angles = positions[:, None] * frequency[None, :]
    cosine = jnp.cos(angles)[:, None, :]
    sine_part = jnp.sin(angles)[:, None, :]
    lower_half = normed[..., :half_size]
    upper_half = normed[..., half_size:]
    rotated = jnp.concatenate(
        [
            lower_half * cosine - upper_half * sine_part,
            upper_half * cosine + lower_half * sine_part,
        ],
        axis=-1,
    )
    return rotated.reshape(token_count, -1).astype(jnp.bfloat16)


def quantize(weights):
    layer_count, row_count, col_count = weights.shape
    blocks = weights.reshape(layer_count, row_count // BLOCK, BLOCK, col_count // BLOCK, BLOCK)
    block_max = jnp.max(jnp.abs(blocks), axis=(2, 4)).astype(jnp.float32) + 1e-06
    scaled = blocks.astype(jnp.float32) / block_max[:, :, None, :, None]
    return (block_max, scaled.reshape(layer_count, row_count, col_count).astype(jnp.bfloat16))


def body(activations, key_weight, key_gain, span_start, next_weight):
    span_begin = span_start[0]
    tile_count = lax.axis_size("tensor")
    tile_width = key_weight.shape[1] // tile_count
    product = jnp.dot(activations, key_weight, preferred_element_type=jnp.float32)
    summed_all = lax.psum(product.astype(jnp.bfloat16), "tensor").astype(jnp.float32)
    summed = lax.dynamic_slice_in_dim(
        summed_all, lax.axis_index("tensor") * tile_width, tile_width, 1
    )
    new_keys = finish_keys(summed, span_begin, key_gain)
    swapped = lax.all_to_all(next_weight, "tensor", split_axis=2, concat_axis=1, tiled=True)
    gathered = lax.all_gather(swapped, "fsdp", axis=1, tiled=True)
    block_max, next_scaled = quantize(gathered)
    return (new_keys, next_scaled, block_max)


def solution(mesh):
    placed = (
        P("fsdp", "tensor"),
        P("tensor", None),
        P(),
        P("fsdp"),
        P(None, ("fsdp", "tensor"), None),
    )
    return jax.shard_map(
        body,
        mesh=mesh,
        in_specs=placed,
        out_specs=(P("fsdp", "tensor"), P(None, None, "tensor"), P(None, None, "tensor")),
        check_vma=False,
    )
```

profile of v0, /device:TPU:26, one launch (start us, length us, event | category | flops | bytes accessed | tf_op | source)
XLA Modules:
  0.0 242.8 jit_solution(10712822932562738262)
XLA Ops:
  8.0 0.0 copy-start
  8.0 0.0 all-reduce.2.cloned.1.call-start
  8.1 1.7 copy-done
  9.7 7.7 %convolution_convert_fusion = bf16[1536,1024]{1,0:T(8,128)(2,1)} fusion(bf16[1536,1280]{1,0:T(8,128)(2,1)} %param.5, bf16[1280,1024]{1,0:T(8,128)(2,1)S(1)} %copy-done), kind=kOutput, calls=%fused_computation.2 | convolution fusion | flops 4028104704 | bytes 9699328 | tf_op jit(solution)/shard_map/dot_general | solution.py:52
  17.4 0.0 all-reduce.2.cloned.1.call-update
  17.5 0.0 all-gather.2.cloned.1.call-start
  17.5 0.8 copy-done.3
  18.3 0.4 copy.28
  18.8 1.0 reshape.86
  19.8 5.5 %all_to_all.18 = bf16[4,2,5120]{2,1,0:T(2,128)(2,1)S(1)} all-to-all(bf16[4,2,5120]{2,1,0:T(2,128)(2,1)S(1)} %reshape.86), channel_id=1, replica_groups=mesh['fsdp'=64,'tensor'=4] {'tensor'}, dimensions={0} | all-to-all | bytes 163840 | tf_op jit(solution)/shard_map/all_to_all | solution.py:58
  25.3 1.3 reshape.87
  26.7 1.0 copy.29
  27.6 0.0 all-gather.2.cloned.1.call-update
  28.3 2.8 %multiply_cosine_fusion = (f32[1536,64]{1,0:T(8,128)S(1)}, f32[1536,64]{1,0:T(8,128)S(1)}) fusion(f32[64]{0:T(128)S(1)} %multiply_exponential_fusion, f32[1536]{0:T(1024)S(1)} %add_convert_fusion.1), kind=kLoop, calls=%fused_computation.8 | loop fusion | flops 98304 | bytes 792832 | tf_op jit(solution)/shard_map/cos | solution.py:26
  31.1 73.0 %all-reduce.2.cloned.1.call-done = bf16[1536,1024]{1,0:T(8,128)(2,1)} async-done(((bf16[1536,1024]{1,0:T(8,128)(2,1)}), bf16[1536,1024]{1,0:T(8,128)(2,1)}) %all-reduce.2.cloned.1.call-update) | async-done | bytes 3145744 | tf_op jit(solution)/shard_map/psum | solution.py:53
  104.1 2.4 dynamic-slice_convert_fusion
  106.5 2.1 reshape.85
  108.6 2.6 %multiply_reduce_fusion = f32[1536,2]{1,0:T(8,128)S(1)} fusion(f32[1536,2,128]{2,1,0:T(2,128)S(1)} %reshape.85), kind=kLoop, calls=%fused_computation.6 | loop fusion | flops 783360 | bytes 1585152 | tf_op jit(solution)/shard_map/reduce_sum | solution.py:18
  111.3 0.1 add_rsqrt_fusion
  111.4 3.5 %multiply_multiply_fusion = f32[1536,2,128]{2,1,0:T(2,128)S(1)} fusion(f32[1536,2,128]{2,1,0:T(2,128)} %copy-done.2, f32[128]{0:T(128)S(1)} %copy-done.4, f32[1536,2]{1,0:T(8,128)S(1)} %add_rsqrt_fusion), kind=kLoop, calls=%fused_computation.5 | loop fusion | flops 786432 | bytes 3158528 | tf_op jit(solution)/shard_map/mul | solution.py:17
  114.9 2.2 subtract_convert_fusion
  117.1 2.2 pad_maximum_fusion
  119.3 1.0 copy.35
  120.3 54.4 %all-gather.2.cloned.1.call-done = bf16[2,5120,256]{2,0,1:T(2,128)(2,1)} async-done(((bf16[2,80,256]{2,0,1:T(2,128)(2,1)}), bf16[2,5120,256]{2,0,1:T(2,128)(2,1)}) %all-gather.2.cloned.1.call-update) | async-done | bytes 5242896 | tf_op jit(solution)/shard_map/all_gather | solution.py:59
  174.6 7.4 %abs.6 = bf16[2,5120,256]{2,0,1:T(2,128)(2,1)} abs(bf16[2,5120,256]{2,0,1:T(2,128)(2,1)} %all-gather.2.cloned.1.call-done) | non-fusion elementwise | flops 2621440 | bytes 10485760 | tf_op jit(solution)/shard_map/abs | solution.py:43
  182.0 14.2 %abs.7 = bf16[2,40,128,2,128]{4,3,0,2,1:T(2,128)(2,1)} reshape(bf16[2,5120,256]{2,0,1:T(2,128)(2,1)} %abs.6) | data formatting | bytes 10485760 | tf_op jit(solution)/shard_map/abs | solution.py:43
  196.2 6.7 %reduce_max.9 = bf16[2,40,2]{2,0,1:T(2,128)(2,1)S(1)} reduce(bf16[2,40,128,2,128]{4,3,0,2,1:T(2,128)(2,1)} %abs.7, bf16[]{:T(256)} %constant.8.clone.1), dimensions={2,4}, to_apply=%region_2.0 | reduce | flops 2621280 | bytes 5243202 | tf_op jit(solution)/shard_map/reduce_max | solution.py:43
  202.9 0.7 copy.31
  203.6 4.5 %div.19 = f32[2,40,128,2,128]{4,3,0,2,1:T(2,128)} broadcast(f32[2,40,2]{2,0,1:T(2,128)S(1)} %convert_add_fusion), dimensions={0,1,3} | broadcast | bytes 10486400 | tf_op jit(solution)/shard_map/div | solution.py:44
  208.1 16.2 %div.20 = f32[2,5120,256]{2,0,1:T(2,128)} reshape(f32[2,40,128,2,128]{4,3,0,2,1:T(2,128)} %div.19) | data formatting | bytes 20971520 | tf_op jit(solution)/shard_map/div | solution.py:44
  224.3 8.0 %fusion = bf16[2,5120,256]{2,0,1:T(2,128)(2,1)S(1)} fusion(f32[2,5120,256]{2,0,1:T(2,128)} %div.20, bf16[2,5120,256]{2,0,1:T(2,128)(2,1)} %all-gather.2.cloned.1.call-done), kind=kLoop, calls=%fused_computation.1 | loop fusion | flops 7864320 | bytes 20971520 | tf_op jit(solution)/shard_map/convert_element_type | solution.py:45
  232.3 3.0 %copy.30 = bf16[2,5120,256]{2,1,0:T(8,128)(2,1)} copy(bf16[2,5120,256]{2,0,1:T(2,128)(2,1)S(1)} %fusion) | data formatting | bytes 10485760
  (10 shorter events, 0.1 us)
Async XLA Ops:
  8.0 1.7 copy-start
  8.0 96.1 %all-reduce.2.cloned.1.call-start = ((), (), s32[]{:S(2)}) async-start(), calls=%async_computation.1 | async-start | bytes 6291456 | tf_op jit(solution)/shard_map/psum | solution.py:53
  17.4 0.9 copy-start.3
  17.5 157.2 %all-gather.2.cloned.1.call-start = ((), (), s32[]{:S(2)}) async-start(), calls=%async_computation.2 | async-start | bytes 5324800 | tf_op jit(solution)/shard_map/all_gather | solution.py:59
  108.6 2.7 %copy-start.2 = (f32[1536,2,128]{2,1,0:T(2,128)}, f32[1536,2,128]{2,1,0:T(2,128)S(1)}, u32[]{:S(2)}) copy-start(f32[1536,2,128]{2,1,0:T(2,128)S(1)} %reshape.85) | copy-start | bytes 4718596
  108.6 2.8 %copy-start.4 = (f32[128]{0:T(128)S(1)}, f32[128]{0:T(128)}, u32[]{:S(2)}) copy-start(f32[128]{0:T(128)} %param.7) | copy-start | bytes 1540
  232.3 3.0 %copy-start.1 = (bf16[1280,1024]{1,0:T(8,128)(2,1)S(1)}, bf16[1280,1024]{1,0:T(8,128)(2,1)}, u32[]{:S(2)}) copy-start(bf16[1280,1024]{1,0:T(8,128)(2,1)} %param.6) | copy-start | bytes 7864324
Sparse Core Ops, SparseCore 0:
  17.6 86.4 all-reduce.1
Sparse Core Ops, SparseCore 1:
  27.7 146.8 all-gather.1
where the time goes:
time: 245 us; the launch traced here: 243 us
  waiting for transfers between devices  127 us (52%)
  local copies, waits for them, and re-layouts  47.9 us (20%)
  other arithmetic  37.9 us (15%)
  between operations  16.3 us (7%)
  matrix products  7.7 us (3%)
  blocking collectives  5.54 us (2%)
    psum x1, waiting for transfers between devices, body(): lax.psum(product.astype(jnp.bfloat16), 'tensor').astype(jnp.float32)  73 us
    all_gather x1, waiting for transfers between devices, body(): gathered = lax.all_gather(swapped, 'fsdp', axis=1, tiled=True)  54.4 us
    div x2, local copies, waits for them, and re-layouts, quantize(): scaled = blocks.astype(jnp.float32) / block_max[:, :, None, :, None]  20.7 us
    abs x1, local copies, waits for them, and re-layouts, quantize(): jnp.abs(blocks)  14.2 us
    unnamed x16, local copies, waits for them, and re-layouts  9.98 us
    convert_element_type x1, other arithmetic, quantize(): scaled.reshape(layer_count, row_count, col_count).astype(jnp.bfloat16)  8.02 us
    dot_general x1, matrix products, body(): jnp.dot(activations, key_weight, preferred_element_type=jnp.float32)  7.7 us
    abs x1, other arithmetic, quantize(): jnp.abs(blocks)  7.39 us
  transfers between devices with their start and end apart: 2, of which 2 were waited for; matrix products, arithmetic and copies ran while one was open for 9% of the time, Pallas kernels for 0%

commit v1 on v0

v1 whole, which is shorter than its diff:
```python
import functools
import math

import jax
import jax.numpy as jnp
from jax import lax
from jax.experimental import pallas as pl
from jax.experimental.pallas import tpu as pltpu
from jax.sharding import Mesh
from jax.sharding import PartitionSpec as P

BLOCK = 128
AXES = ("y", "xh", "z", "xl", "c")
SIZES = (4, 2, 8, 2, 2)
F32 = jnp.float32
BF16 = jnp.bfloat16
VMEM_LIMIT = 48 * 1024 * 1024


def shift(x, axis, step):
    n = SIZES[AXES.index(axis)]
    return lax.ppermute(x, axis, [(i, (i + step) % n) for i in range(n)])


def call(kernel, out_shape, flops=0, nbytes=0, **kw):
    return pl.pallas_call(
        kernel,
        out_shape=out_shape,
        compiler_params=pltpu.CompilerParams(vmem_limit_bytes=VMEM_LIMIT),
        cost_estimate=pl.CostEstimate(flops=flops, bytes_accessed=nbytes, transcendentals=0),
        **kw,
    )


def project_kernel(idx, a, w, out):
    out[...] = jnp.dot(a[...], w[...], preferred_element_type=F32).astype(out.dtype)


def project_add_kernel(idx, a, w, r, out):
    s = jnp.dot(a[...], w[...], preferred_element_type=F32)
    out[...] = (s + r[...].astype(F32)).astype(out.dtype)


def project_two_kernel(idx, a, w, v, out, own):
    x = a[...]
    out[...] = jnp.dot(x, w[...], preferred_element_type=F32).astype(out.dtype)
    own[...] = jnp.dot(x, v[...], preferred_element_type=F32)


def project(kernel, a, w, tiles, extra, outs, rows=512):
    t, d = a.shape
    width = w.shape[1] // 4
    tile_specs = [
        pl.BlockSpec((d, width), functools.partial(lambda i, idx, k: (0, idx[k]), k=k))
        for k in range(len(tiles))
    ]
    row_spec = pl.BlockSpec((rows, width), lambda i, idx: (i, 0))
    return call(
        kernel,
        [jax.ShapeDtypeStruct((t, width), dt) for dt in outs],
        flops=2 * t * d * width * len(tiles),
        nbytes=2 * t * d + 2 * d * width * len(tiles) + 4 * t * width,
        grid_spec=pltpu.PrefetchScalarGridSpec(
            num_scalar_prefetch=1,
            grid=(t // rows,),
            in_specs=[pl.BlockSpec((rows, d), lambda i, idx: (i, 0))]
            + tile_specs
            + [row_spec] * len(extra),
            out_specs=[row_spec] * len(outs),
        ),
    )(jnp.stack(tiles).astype(jnp.int32), a, *([w] * len(tiles)), *extra)


def finish_kernel(own, r, q, gain, cosine, sine, out):
    g = gain[...]
    c = cosine[...]
    s = sine[...]
    for h in range(2):
        at = slice(h * 128, (h + 1) * 128)
        x = own[:, at] + r[:, at].astype(F32) + q[:, at].astype(F32)
        n = x * lax.rsqrt(jnp.mean(x * x, axis=-1, keepdims=True) + 1e-06) * g
        out[:, at] = (n * c + pltpu.roll(n, 64, 1) * s).astype(BF16)


def finish(own, r, q, gain, cosine, sine, rows=512):
    t, width = own.shape
    wide = pl.BlockSpec((rows, width), lambda i: (i, 0))
    narrow = pl.BlockSpec((rows, 128), lambda i: (i, 0))
    return call(
        finish_kernel,
        jax.ShapeDtypeStruct((t, width), BF16),
        flops=20 * t * width,
        nbytes=16 * t * width,
        grid=(t // rows,),
        in_specs=[wide, wide, wide, pl.BlockSpec((1, 128), lambda i: (0, 0)), narrow, narrow],
        out_specs=wide,
    )(own, r, q, gain.reshape(1, 128), cosine, sine)


def tables(span_begin, t):
    positions = (span_begin + jnp.arange(t, dtype=jnp.int32)).astype(F32)
    lane = jnp.arange(128, dtype=jnp.int32)
    frequency = jnp.exp((lane % 64).astype(F32) * (-2.0 * math.log(1000000.0) / 128))
    angles = positions[:, None] * frequency[None, :]
    sign = jnp.where(lane < 64, -1.0, 1.0).astype(F32)
    return jnp.cos(angles), jnp.sin(angles) * sign[None, :]


def split_kernel(w, out):
    for xh in range(2):
        for t in range(4):
            out[xh * 4 + t] = w[:, :, t * 256 : (t + 1) * 256]


def merge_kernel(x, *outs):
    for layer in range(2):
        for xh in range(2):
            parts = [x[xh * 4 + t, layer].astype(F32) for t in range(4)]
            outs[layer][xh] = jnp.concatenate(parts, axis=0).astype(BF16)


def place_rows_kernel(z, *refs):
    out = refs[-1]
    for d, ref in enumerate(refs[:-1]):
        at = pl.multiple_of(lax.rem(z[0] + d, 8) * 80, 16)
        out[:, pl.ds(at, 80), :] = ref[...]


def place_lead_kernel(y, *refs):
    out = refs[-1]
    for d, ref in enumerate(refs[:-1]):
        out[lax.rem(y[0] + d, 4)] = ref[...]


SMEM = pl.BlockSpec(memory_space=pltpu.SMEM)
VMEM = pl.BlockSpec(memory_space=pltpu.VMEM)


def place(kernel, index, pieces, shape):
    return call(
        kernel,
        jax.ShapeDtypeStruct(shape, BF16),
        nbytes=4 * math.prod(shape),
        in_specs=[SMEM] + [VMEM] * len(pieces),
        out_specs=VMEM,
    )(index, *pieces)


def scale_unit(x, first, put, bm):
    lane = lax.broadcasted_iota(jnp.int32, (1, 128), 1)
    for j in range(2):
        row = bm[j : j + 1, :]
        for k in range(5):
            blk = x[k * 128 : (k + 1) * 128, j * 128 : (j + 1) * 128]
            m = jnp.max(jnp.abs(blk).astype(F32), axis=(0, 1), keepdims=True) + 1e-06
            put(k, j, (blk.astype(F32) * (1.0 / m)).astype(BF16))
            row = jnp.where(lane == first + k, m, row)
        bm[j : j + 1, :] = row


def scale_groups_kernel(units, n, idx, *refs):
    ins, out, bm = refs[:n], refs[-2], refs[-1]
    i = pl.program_id(0)

    @pl.when(i == 0)
    def _():
        bm[...] = refs[n][...]

    for u, (k, xh) in enumerate(units):

        @pl.when(i == u)
        def _(k=k, xh=xh):
            x = ins[k][...] if xh is None else ins[k][xh]

            def put(r, j, v):
                out[0, r * 128 : (r + 1) * 128, j * 128 : (j + 1) * 128] = v

            scale_unit(x, idx[i] * 5, put, bm)


def scale_groups(pieces, groups, bm, buffer):
    units = []
    for k, p in enumerate(pieces):
        units += [(k, None)] if p.ndim == 2 else [(k, xh) for xh in range(p.shape[0])]
    n = len(pieces)
    ins = list(pieces) + [bm]
    in_specs = [
        pl.BlockSpec(p.shape, functools.partial(lambda i, idx, nd: (0,) * nd, nd=p.ndim))
        for p in ins
    ]
    alias = {}
    if buffer is not None:
        ins.append(buffer)
        in_specs.append(pl.BlockSpec(memory_space=pl.ANY))
        alias = {n + 2: 0}
    return call(
        functools.partial(scale_groups_kernel, units, n),
        [jax.ShapeDtypeStruct((2, 5120, 256), BF16), jax.ShapeDtypeStruct((2, 128), F32)],
        flops=len(units) * 640 * 256 * 8,
        nbytes=len(units) * 640 * 256 * 4,
        grid_spec=pltpu.PrefetchScalarGridSpec(
            num_scalar_prefetch=1,
            grid=(len(units),),
            in_specs=in_specs,
            out_specs=[
                pl.BlockSpec((1, 640, 256), lambda i, idx: (0, idx[i], 0)),
                pl.BlockSpec((2, 128), lambda i, idx: (0, 0)),
            ],
        ),
        input_output_aliases=alias,
    )(jnp.stack(groups).astype(jnp.int32), *ins)


def ring_kernel(z, *refs):
    pieces, low, high, bma, _, out, bm, held, acc = (
        refs[:7], refs[7], refs[8], refs[9], refs[10], refs[11], refs[12], refs[13], refs[14]
    )
    i = pl.program_id(0)

    @pl.when(i == 0)
    def _():
        acc[...] = jnp.zeros_like(acc)

    for xh in range(2):
        for d, ref in enumerate(pieces):
            at = pl.multiple_of(lax.rem(z[0] + z[1 + d], 8) * 80, 16)
            held[pl.ds(at, 80), :] = ref[0, xh]
        at = pl.multiple_of(lax.rem(z[0] + 4, 8) * 80, 16)

        @pl.when(i < 2)
        def _():
            held[pl.ds(at, 80), :] = low[0, xh]

        @pl.when(i >= 2)
        def _():
            held[pl.ds(at, 80), :] = high[0, xh]

        def put(r, j, v):
            out[0, xh * 640 + r * 128 : xh * 640 + (r + 1) * 128, j * 128 : (j + 1) * 128] = v

        scale_unit(held, (i * 2 + xh) * 5, put, acc)

    @pl.when(i == 3)
    def _():
        bm[0] = bma[:, :40]
        bm[1] = acc[:, :40]


def scale_ring(z0, pieces, offsets, low, high, bma, buffer):
    whole = pl.BlockSpec((1, 2, 80, 256), lambda i, z: (i, 0, 0, 0))
    return call(
        ring_kernel,
        [jax.ShapeDtypeStruct((2, 5120, 256), BF16), jax.ShapeDtypeStruct((2, 2, 40), F32)],
        flops=5120 * 256 * 8,
        nbytes=5120 * 256 * 4,
        grid_spec=pltpu.PrefetchScalarGridSpec(
            num_scalar_prefetch=1,
            grid=(4,),
            in_specs=[whole] * 7
            + [
                pl.BlockSpec((1, 2, 80, 256), lambda i, z: (jnp.minimum(i, 1), 0, 0, 0)),
                pl.BlockSpec((1, 2, 80, 256), lambda i, z: (jnp.maximum(i - 2, 0), 0, 0, 0)),
                pl.BlockSpec((2, 128), lambda i, z: (0, 0)),
                pl.BlockSpec(memory_space=pl.ANY),
            ],
            out_specs=[
                pl.BlockSpec((1, 1280, 256), lambda i, z: (1, i, 0)),
                pl.BlockSpec((2, 2, 40), lambda i, z: (0, 0, 0)),
            ],
            scratch_shapes=[pltpu.VMEM((640, 256), BF16), pltpu.VMEM((2, 128), F32)],
        ),
        input_output_aliases={11: 0},
    )(jnp.stack([z0] + [jnp.int32(o) for o in offsets]), *pieces, low, high, bma, buffer)


def body(activations, key_weight, key_gain, span_start, next_weight):
    y0, z0 = lax.axis_index("y"), lax.axis_index("z")
    xl, c = lax.axis_index("xl"), lax.axis_index("c")

    spread = call(
        split_kernel,
        jax.ShapeDtypeStruct((8, 2, 20, 256), BF16),
        nbytes=4 * 8 * 2 * 20 * 256,
        in_specs=[VMEM],
        out_specs=VMEM,
    )(next_weight)
    line = lax.all_to_all(spread, ("xh", "xl", "c"), split_axis=0, concat_axis=0, tiled=True)
    a0, b0 = call(
        merge_kernel,
        [jax.ShapeDtypeStruct((2, 80, 256), BF16)] * 2,
        nbytes=4 * 8 * 2 * 20 * 256,
        in_specs=[VMEM],
        out_specs=[VMEM] * 2,
    )(line)

    by = [b0, shift(b0, "y", -1), shift(b0, "y", 2), shift(b0, "y", 1)]
    mb = place(place_lead_kernel, y0.reshape(1), by, (4, 2, 80, 256))
    az = {0: a0}
    for d in (1, 2, 3):
        az[d] = shift(az[d - 1], "z", -1)
        az[8 - d] = shift(az[(9 - d) % 8], "z", 1)
    az[4] = shift(az[3], "z", -1)
    ma = place(place_rows_kernel, z0.reshape(1), [az[d] for d in range(8)], (2, 640, 256))

    bz = {0: mb}
    for d in (1, 2, 3):
        bz[d] = shift(bz[d - 1], "z", -1)
        bz[8 - d] = shift(bz[(9 - d) % 8], "z", 1)
    low = shift(bz[3][:2], "z", -1)
    high = shift(bz[5][2:], "z", 1)

    up, down = shift(ma, "y", -1), shift(ma, "y", 1)
    far0 = shift(up[0], "y", -1)
    far1 = shift(down[1], "y", 1)

    far, near = (1 - xl) * 2, xl * 2
    (p1,) = project(project_kernel, activations, key_weight, [far + 1 - c], [], [BF16])
    r1 = shift(p1, "c", 1)
    (p2,) = project(project_add_kernel, activations, key_weight, [far + c], [r1], [BF16])
    r2 = shift(p2, "xl", 1)
    p3, own = project(
        project_two_kernel, activations, key_weight, [near + 1 - c, near + c], [], [BF16, F32]
    )
    r3 = shift(p3, "c", 1)
    cosine, sine = tables(span_start[0], activations.shape[0])
    new_keys = finish(own, r3, r2, key_gain, cosine, sine)

    g = lambda d: lax.rem(y0 + d, 4) * 2
    bm = jnp.zeros((2, 128), F32)
    buf, bm = scale_groups([ma], [g(0), g(0) + 1], bm, None)
    buf, bm = scale_groups([up, down], [g(1), g(1) + 1, g(3), g(3) + 1], bm, buf)
    buf, bm = scale_groups([far0, far1], [g(2), g(2) + 1], bm, buf)
    order = [0, 1, 7, 2, 6, 3, 5]
    next_scaled, block_max = scale_ring(
        z0, [bz[d] for d in order], order, low, high, bm, buf
    )
    return new_keys, next_scaled, block_max.transpose(0, 2, 1)


def solution(mesh):
    line = Mesh(mesh.devices.reshape(SIZES), AXES)
    fsdp, tensor = ("y", "xh", "z"), ("xl", "c")
    placed = (
        P(fsdp, tensor),
        P(tensor, None),
        P(),
        P(fsdp),
        P(None, fsdp + tensor, None),
    )
    return jax.shard_map(
        body,
        mesh=line,
        in_specs=placed,
        out_specs=(P(fsdp, tensor), P(None, None, tensor), P(None, None, tensor)),
        check_vma=False,
    )
```

time: 245 us -> 104 us (0.42)
  waiting for transfers between devices: 127 us -> 10.1 us
  local copies, waits for them, and re-layouts: 47.9 us -> 6.33 us
  starting transfers between devices: 0.08 us -> 35.2 us
  Pallas kernels: 0 us -> 35.1 us
  other arithmetic: 37.9 us -> 4.14 us
  between operations: 16.3 us -> 1.43 us
  matrix products: 7.7 us -> 0 us
  blocking collectives: 5.54 us -> 9.66 us
    psum x1 -> x0, waiting for transfers between devices: 73 us -> none  [body(): lax.psum(product.astype(jnp.bfloat16), 'tensor').astype(jnp.float32)]
    all_gather x1 -> x0, waiting for transfers between devices: 54.4 us -> none  [body(): gathered = lax.all_gather(swapped, 'fsdp', axis=1, tiled=True)]
    ppermute x0 -> x25, starting transfers between devices: none -> 35.2 us  [shift(): return lax.ppermute(x, axis, [(i, (i + step) % n) for i in range(n)])]
    pallas_call x0 -> x12, Pallas kernels: none -> 35.1 us  [the longest x3 15.5 us: project(): call(kernel, [jax.ShapeDtypeStruct((t, width), dt) for dt in outs], flops...]
    div x2 -> x0, local copies, waits for them, and re-layouts: 20.7 us -> none  [quantize(): scaled = blocks.astype(jnp.float32) / block_max[:, :, None, :, None]]
    abs x1 -> x0, local copies, waits for them, and re-layouts: 14.2 us -> none  [quantize(): jnp.abs(blocks)]
    convert_element_type x3 -> x1, other arithmetic: 10.4 us -> 0.01 us  [tables(): positions = (span_begin + jnp.arange(t, dtype=jnp.int32)).astype(F32)]
    ppermute x0 -> x25, waiting for transfers between devices: none -> 10.1 us  [shift(): return lax.ppermute(x, axis, [(i, (i + step) % n) for i in range(n)])]
  transfers between devices with their start and end apart: 2 -> 25, of which waited for: 2 -> 6; matrix products, arithmetic and copies ran while one was open for 9% -> 8% of each run, Pallas kernels for 0% -> 31%
where the time goes in v1:
time: 104 us; the launch traced here: 102 us
  starting transfers between devices  35.2 us (34%)
  Pallas kernels  35.1 us (34%)
  waiting for transfers between devices  10.1 us (10%)
  blocking collectives  9.66 us (9%)
  local copies, waits for them, and re-layouts  6.33 us (6%)
  other arithmetic  4.14 us (4%)
  between operations  1.43 us (1%)
    ppermute x25, starting transfers between devices, shift(): return lax.ppermute(x, axis, [(i, (i + step) % n) for i in range(n)])  35.2 us
    pallas_call x3, Pallas kernels, project(): call(kernel, [jax.ShapeDtypeStruct((t, width), dt) for dt in outs], flops...  15.5 us
    ppermute x25, waiting for transfers between devices, shift(): return lax.ppermute(x, axis, [(i, (i + step) % n) for i in range(n)])  10.1 us
    all_to_all x1, blocking collectives, body(): lax.all_to_all(spread, ('xh', 'xl', 'c'), split_axis=0, concat_axis=0, ti...  9.66 us
    pallas_call x3, Pallas kernels, scale_groups(): call(functools.partial(scale_groups_kernel, units, n), [jax.ShapeDtypeStr...  8.79 us
    pallas_call x1, Pallas kernels, scale_ring(): call(ring_kernel, [jax.ShapeDtypeStruct((2, 5120, 256), BF16), jax.ShapeD...  5.52 us
    mul x1, other arithmetic, tables(): return (jnp.cos(angles), jnp.sin(angles) * sign[None, :])  3.83 us
    pallas_call x1, Pallas kernels, finish(): call(finish_kernel, jax.ShapeDtypeStruct((t, width), BF16), flops=20 * t...  3.57 us
  transfers between devices with their start and end apart: 25, of which 6 were waited for; matrix products, arithmetic and copies ran while one was open for 8% of the time, Pallas kernels for 31%

profile of v1, /device:TPU:26, one launch (start us, length us, event | category | flops | bytes accessed | tf_op | source)
XLA Modules:
  0.0 101.9 jit_solution(11344843929342783208)
XLA Ops:
  0.6 0.9 copy.12.w
  1.7 9.7 %all_to_all.5 = bf16[8,2,20,256]{3,1,2,0:T(2,128)(2,1)S(1)} all-to-all(bf16[8,2,20,256]{3,1,2,0:T(2,128)(2,1)S(1)} %copy.13), channel_id=1, replica_groups=mesh['y'=4,'xh'=2,'z'=8,'xl'=2,'c'=2] {'xh','xl','c'}, dimensions={0} | all-to-all | bytes 327680 | tf_op jit(solution)/shard_map/all_to_all | solution.py:287
  11.4 5.9 %collective-permute-start.14 = (bf16[2,80,256]{2,1,0:T(8,128)(2,1)S(1)}, bf16[2,80,256]{2,1,0:T(8,128)(2,1)S(1)}, u32[]{:S(2)}, u32[]{:S(2)}) collective-permute-start(bf16[2,80,256]{2,1,0:T(8,128)(2,1)S(1)} %get-tuple-element.18.refs_0_), channel_id=1, source_target_pairs={{0,28},{4,0},{8,4},{12,8},{16,12},{20,16},{24,20},{28,24},{1,29},{... | collective-permute-start | bytes 245768 | tf_op jit(solution)/shard_map/ppermute | solution.py:22
  18.1 1.3 %collective-permute-done.14.refs_1_ = bf16[2,80,256]{2,1,0:T(8,128)(2,1)S(1)} collective-permute-done((bf16[2,80,256]{2,1,0:T(8,128)(2,1)S(1)}, bf16[2,80,256]{2,1,0:T(8,128)(2,1)S(1)}, u32[]{:S(2)}, u32[]{:S(2)}) %collective-permute-start.14) | collective-permute-done | bytes 81952 | tf_op jit(solution)/shard_map/ppermute | solution.py:22
  19.4 3.6 %collective-permute-start.15 = (bf16[2,80,256]{2,1,0:T(8,128)(2,1)S(1)}, bf16[2,80,256]{2,1,0:T(8,128)(2,1)S(1)}, u32[]{:S(2)}, u32[]{:S(2)}) collective-permute-start(bf16[2,80,256]{2,1,0:T(8,128)(2,1)S(1)} %collective-permute-done.14.refs_1_), channel_id=1, source_target_pairs={{0,28},{4,0},{8,4},{12,8},{16,12},{20,16},{24,20},{28,24},{1,29},{... | collective-permute-start | bytes 245768 | tf_op jit(solution)/shard_map/ppermute | solution.py:22
  23.7 1.3 %collective-permute-done.15.refs_2_ = bf16[2,80,256]{2,1,0:T(8,128)(2,1)S(1)} collective-permute-done((bf16[2,80,256]{2,1,0:T(8,128)(2,1)S(1)}, bf16[2,80,256]{2,1,0:T(8,128)(2,1)S(1)}, u32[]{:S(2)}, u32[]{:S(2)}) %collective-permute-start.15) | collective-permute-done | bytes 81952 | tf_op jit(solution)/shard_map/ppermute | solution.py:22
  25.1 3.6 %collective-permute-start.16 = (bf16[2,80,256]{2,1,0:T(8,128)(2,1)S(1)}, bf16[2,80,256]{2,1,0:T(8,128)(2,1)S(1)}, u32[]{:S(2)}, u32[]{:S(2)}) collective-permute-start(bf16[2,80,256]{2,1,0:T(8,128)(2,1)S(1)} %collective-permute-done.15.refs_2_), channel_id=1, source_target_pairs={{0,28},{4,0},{8,4},{12,8},{16,12},{20,16},{24,20},{28,24},{1,29},{... | collective-permute-start | bytes 245768 | tf_op jit(solution)/shard_map/ppermute | solution.py:22
  29.4 0.9 collective-permute-start.4
  30.4 2.2 %collective-permute-start.5 = (bf16[2,80,256]{2,1,0:T(8,128)(2,1)S(1)}, bf16[2,80,256]{2,1,0:T(8,128)(2,1)S(1)}, u32[]{:S(2)}, u32[]{:S(2)}) collective-permute-start(bf16[2,80,256]{2,1,0:T(8,128)(2,1)S(1)} %get-tuple-element.17.refs_0_), channel_id=1, source_target_pairs={{0,64},{64,128},{128,192},{192,0},{1,65},{65,129},{129,193},{193,1... | collective-permute-start | bytes 245768 | tf_op jit(solution)/shard_map/ppermute | solution.py:22
  32.5 3.2 %collective-permute-start.17 = (bf16[2,80,256]{2,1,0:T(8,128)(2,1)S(1)}, bf16[2,80,256]{2,1,0:T(8,128)(2,1)S(1)}, u32[]{:S(2)}, u32[]{:S(2)}) collective-permute-start(bf16[2,80,256]{2,1,0:T(8,128)(2,1)S(1)} %collective-permute-done.16.refs_3_), channel_id=1, source_target_pairs={{0,28},{4,0},{8,4},{12,8},{16,12},{20,16},{24,20},{28,24},{1,29},{... | collective-permute-start | bytes 245768 | tf_op jit(solution)/shard_map/ppermute | solution.py:22
  35.8 1.7 %copy-done = bf16[1280,1024]{1,0:T(8,128)(2,1)S(1)} copy-done((bf16[1280,1024]{1,0:T(8,128)(2,1)S(1)}, bf16[1280,1024]{1,0:T(8,128)(2,1)}, u32[]{:S(2)}) %copy-start) | copy-done | bytes 2621464
  37.5 4.6 %shard_map.77 = bf16[1536,256]{1,0:T(8,128)(2,1)} custom-call(s32[1]{0:T(128)} %bitcast.3.idx, bf16[1536,1280]{1,0:T(8,128)(2,1)} %a.5, bf16[1280,1024]{1,0:T(8,128)(2,1)S(1)} %copy-done), custom_call_target="tpu_custom_call" | custom-call | flops 1006632960 | bytes 6160384 | tf_op jit(solution)/shard_map/pallas_call | solution.py:58
  42.9 2.0 %collective-permute-start.7 = (bf16[4,2,80,256]{3,2,1,0:T(8,128)(2,1)}, bf16[4,2,80,256]{3,2,1,0:T(8,128)(2,1)}, u32[]{:S(2)}, u32[]{:S(2)}) collective-permute-start(bf16[4,2,80,256]{3,2,1,0:T(8,128)(2,1)} %shard_map.82.refs_0_), channel_id=1, source_target_pairs={{0,4},{4,8},{8,12},{12,16},{16,20},{20,24},{24,28},{28,0},{1,5},{5... | collective-permute-start | bytes 983048 | tf_op jit(solution)/shard_map/ppermute | solution.py:22
  44.9 0.9 shard_map.83.refs_0_
  46.1 3.0 %collective-permute-start.23 = (bf16[2,640,256]{2,1,0:T(8,128)(2,1)}, bf16[2,640,256]{2,1,0:T(8,128)(2,1)}, u32[]{:S(2)}, u32[]{:S(2)}) collective-permute-start(bf16[2,640,256]{2,1,0:T(8,128)(2,1)} %shard_map.83.refs_0_), channel_id=1, source_target_pairs={{0,64},{64,128},{128,192},{192,0},{1,65},{65,129},{129,193},{193,1... | collective-permute-start | bytes 1966088 | tf_op jit(solution)/shard_map/ppermute | solution.py:22
  49.1 3.8 %fusion = (f32[1536,128]{1,0:T(8,128)S(1)}, f32[1536,128]{1,0:T(8,128)}) fusion(f32[128]{0:T(128)S(1)} %get-tuple-element.29, f32[128]{0:T(128)S(1)} %get-tuple-element.30, f32[1536]{0:T(1024)S(1)} %add_convert_fusion), kind=kLoop, calls=%fused_computation.2 | loop fusion | flops 393216 | bytes 1580032 | tf_op jit(solution)/shard_map/mul | solution.py:106
  53.3 1.5 %collective-permute-start.8 = (bf16[4,2,80,256]{3,2,1,0:T(8,128)(2,1)}, bf16[4,2,80,256]{3,2,1,0:T(8,128)(2,1)}, u32[]{:S(2)}, u32[]{:S(2)}) collective-permute-start(bf16[4,2,80,256]{3,2,1,0:T(8,128)(2,1)} %collective-permute-done.6.refs_1_), channel_id=1, source_target_pairs={{0,28},{4,0},{8,4},{12,8},{16,12},{20,16},{24,20},{28,24},{1,29},{... | collective-permute-start | bytes 983048 | tf_op jit(solution)/shard_map/ppermute | solution.py:22
  55.4 5.7 %shard_map.76 = (bf16[1536,256]{1,0:T(8,128)(2,1)}, f32[1536,256]{1,0:T(8,128)S(1)}) custom-call(s32[2]{0:T(128)S(1)} %pad_add_fusion.idx, bf16[1536,1280]{1,0:T(8,128)(2,1)} %a.5, bf16[1280,1024]{1,0:T(8,128)(2,1)S(1)} %copy-done.1, bf16[1280,1024]{1,0:T(8,128)(2,1)S(1)} %copy-done.1), custom_call_target="tpu_custom_call" | custom-call | flops 2013265920 | bytes 6815744 | tf_op jit(solution)/shard_map/pallas_call | solution.py:58
  61.2 5.2 %shard_map.78 = bf16[1536,256]{1,0:T(8,128)(2,1)} custom-call(s32[1]{0:T(128)} %bitcast.2.idx, bf16[1536,1280]{1,0:T(8,128)(2,1)} %a.5, bf16[1280,1024]{1,0:T(8,128)(2,1)S(1)} %copy-done.1, bf16[1536,256]{1,0:T(8,128)(2,1)} %collective-permute-done.1.r), custom_call_target="tpu_custom_call" | custom-call | flops 1006632960 | bytes 6160384 | tf_op jit(solution)/shard_map/pallas_call | solution.py:58
  66.3 1.5 %collective-permute-start.2 = (bf16[1536,256]{1,0:T(8,128)(2,1)}, bf16[1536,256]{1,0:T(8,128)(2,1)S(1)}, u32[]{:S(2)}, u32[]{:S(2)}) collective-permute-start(bf16[1536,256]{1,0:T(8,128)(2,1)} %shard_map.78), channel_id=1, source_target_pairs={{0,2},{2,0},{1,3},{3,1},{4,6},{6,4},{5,7},{7,5},{8,10},{10,8},{9,1... | collective-permute-start | bytes 2359304 | tf_op jit(solution)/shard_map/ppermute | solution.py:22
  67.9 2.7 %collective-permute-start.10 = (bf16[4,2,80,256]{3,2,1,0:T(8,128)(2,1)}, bf16[4,2,80,256]{3,2,1,0:T(8,128)(2,1)S(1)}, u32[]{:S(2)}, u32[]{:S(2)}) collective-permute-start(bf16[4,2,80,256]{3,2,1,0:T(8,128)(2,1)} %collective-permute-done.8.refs_3_), channel_id=1, source_target_pairs={{0,28},{4,0},{8,4},{12,8},{16,12},{20,16},{24,20},{28,24},{1,29},{... | collective-permute-start | bytes 983048 | tf_op jit(solution)/shard_map/ppermute | solution.py:22
  70.6 1.0 slice_bitcast_fusion.1
  71.9 1.7 %slice_bitcast_fusion = bf16[640,256]{1,0:T(8,128)(2,1)} fusion(bf16[2,640,256]{2,1,0:T(8,128)(2,1)} %collective-permute-done.23.refs_1_), kind=kLoop, calls=%fused_computation.3 | loop fusion | bytes 655360 | tf_op jit(solution)/shard_map/squeeze | solution.py:314
  73.6 4.0 %collective-permute-done.10.refs_5_ = bf16[4,2,80,256]{3,2,1,0:T(8,128)(2,1)S(1)} collective-permute-done((bf16[4,2,80,256]{3,2,1,0:T(8,128)(2,1)}, bf16[4,2,80,256]{3,2,1,0:T(8,128)(2,1)S(1)}, u32[]{:S(2)}, u32[]{:S(2)}) %collective-permute-start.10) | collective-permute-done | bytes 327712 | tf_op jit(solution)/shard_map/ppermute | solution.py:22
  77.7 1.0 collective-permute-start.24
  78.7 2.2 %collective-permute-done.11.refs_6_ = bf16[4,2,80,256]{3,2,1,0:T(8,128)(2,1)S(1)} collective-permute-done((bf16[4,2,80,256]{3,2,1,0:T(8,128)(2,1)}, bf16[4,2,80,256]{3,2,1,0:T(8,128)(2,1)S(1)}, u32[]{:S(2)}, u32[]{:S(2)}) %collective-permute-start.11) | collective-permute-done | bytes 327712 | tf_op jit(solution)/shard_map/ppermute | solution.py:22
  81.0 1.4 %collective-permute-start.12 = (bf16[2,2,80,256]{3,2,1,0:T(8,128)(2,1)S(1)}, bf16[2,2,80,256]{3,2,1,0:T(8,128)(2,1)S(1)}, u32[]{:S(2)}, u32[]{:S(2)}) collective-permute-start(bf16[2,2,80,256]{3,2,1,0:T(8,128)(2,1)S(1)} %slice.16), channel_id=1, source_target_pairs={{0,28},{4,0},{8,4},{12,8},{16,12},{20,16},{24,20},{28,24},{1,29},{... | collective-permute-start | bytes 491528 | tf_op jit(solution)/shard_map/ppermute | solution.py:22
  84.0 2.9 %shard_map.84 = (bf16[2,5120,256]{2,1,0:T(8,128)(2,1)}, f32[2,128]{1,0:T(2,128)S(1)}) custom-call(s32[2]{0:T(128)S(1)} %pad_add_fusion.3.idx, bf16[2,640,256]{2,1,0:T(8,128)(2,1)} %shard_map.83.refs_0_, f32[2,128]{1,0:T(2,128)S(1)} %broadcast_in_dim.16.refs_1_), custom_call_target="tpu_custom_call" | custom-call | flops 2621440 | bytes 1310720 | tf_op jit(solution)/shard_map/pallas_call | solution.py:196
  86.9 4.1 %shard_map.85 = (bf16[2,5120,256]{2,1,0:T(8,128)(2,1)}, f32[2,128]{1,0:T(2,128)S(1)}) custom-call(s32[4]{0:T(128)S(1)} %pad_add_fusion.2.idx, bf16[2,640,256]{2,1,0:T(8,128)(2,1)} %collective-permute-done.21.refs_0_, bf16[2,640,256]{2,1,0:T(8,128)(2,1)} %collective-permute-done.23.refs_1_, ...), custom_call_target="tpu_custom_call", output_to_operand_aliasing={{0}: (4, {})} | custom-call | flops 5242880 | bytes 2621440 | tf_op jit(solution)/shard_map/pallas_call | solution.py:196
  91.0 1.8 %shard_map.86 = (bf16[2,5120,256]{2,1,0:T(8,128)(2,1)}, f32[2,128]{1,0:T(2,128)S(1)}) custom-call(s32[2]{0:T(128)S(1)} %pad_add_fusion.1.idx, bf16[640,256]{1,0:T(8,128)(2,1)S(1)} %collective-permute-done.22.refs_0_, bf16[640,256]{1,0:T(8,128)(2,1)S(1)} %collective-permute-done.24.refs_1_, ...), custom_call_target="tpu_custom_call", output_to_operand_aliasing={{0}: (4, {})} | custom-call | flops 2621440 | bytes 1310720 | tf_op jit(solution)/shard_map/pallas_call | solution.py:196
  92.8 5.5 %shard_map.87 = (bf16[2,5120,256]{2,1,0:T(8,128)(2,1)}, f32[2,2,40]{2,1,0:T(2,128)}) custom-call(s32[8]{0:T(128)S(1)} %stack.60.z, bf16[4,2,80,256]{3,2,1,0:T(8,128)(2,1)} %shard_map.82.refs_0_, bf16[4,2,80,256]{3,2,1,0:T(8,128)(2,1)} %collective-permute-done.6.refs_1_, ...), custom_call_target="tpu_custom_call", output_to_operand_aliasing={{0}: (11, {})} | custom-call | flops 10485760 | bytes 5242880 | tf_op jit(solution)/shard_map/pallas_call | solution.py:251
  98.3 3.6 %shard_map.79 = bf16[1536,256]{1,0:T(8,128)(2,1)} custom-call(f32[1536,256]{1,0:T(8,128)S(1)} %copy-done.4, bf16[1536,256]{1,0:T(8,128)(2,1)} %collective-permute-done.r, bf16[1536,256]{1,0:T(8,128)(2,1)S(1)} %collective-permute-done.2.q, f32[1,128]{1,0:T(1,128)S(1)} %bitcast.22, f32[1536,128]{1,0:T(8,128)S(1)} %copy-done.2, ...), custom_call_target="tpu_custom_call" | custom-call | flops 7864320 | bytes 6291456 | tf_op jit(solution)/shard_map/pallas_call | solution.py:89
  (59 shorter events, 5.8 us)
Async XLA Ops:
  11.4 8.0 %collective-permute-start.14 = (bf16[2,80,256]{2,1,0:T(8,128)(2,1)S(1)}, bf16[2,80,256]{2,1,0:T(8,128)(2,1)S(1)}, u32[]{:S(2)}, u32[]{:S(2)}) collective-permute-start(bf16[2,80,256]{2,1,0:T(8,128)(2,1)S(1)} %get-tuple-element.18.refs_0_), channel_id=1, source_target_pairs={{0,28},{4,0},{8,4},{12,8},{16,12},{20,16},{24,20},{28,24},{1,29},{... | collective-permute-start | bytes 245768 | tf_op jit(solution)/shard_map/ppermute | solution.py:22
  18.0 5.7 %collective-permute-start.18 = (bf16[2,80,256]{2,1,0:T(8,128)(2,1)S(1)}, bf16[2,80,256]{2,1,0:T(8,128)(2,1)S(1)}, u32[]{:S(2)}, u32[]{:S(2)}) collective-permute-start(bf16[2,80,256]{2,1,0:T(8,128)(2,1)S(1)} %get-tuple-element.18.refs_0_), channel_id=1, source_target_pairs={{0,4},{4,8},{8,12},{12,16},{16,20},{20,24},{24,28},{28,0},{1,5},{5... | collective-permute-start | bytes 245768 | tf_op jit(solution)/shard_map/ppermute | solution.py:22
  19.4 5.7 %collective-permute-start.15 = (bf16[2,80,256]{2,1,0:T(8,128)(2,1)S(1)}, bf16[2,80,256]{2,1,0:T(8,128)(2,1)S(1)}, u32[]{:S(2)}, u32[]{:S(2)}) collective-permute-start(bf16[2,80,256]{2,1,0:T(8,128)(2,1)S(1)} %collective-permute-done.14.refs_1_), channel_id=1, source_target_pairs={{0,28},{4,0},{8,4},{12,8},{16,12},{20,16},{24,20},{28,24},{1,29},{... | collective-permute-start | bytes 245768 | tf_op jit(solution)/shard_map/ppermute | solution.py:22
  23.7 8.8 %collective-permute-start.19 = (bf16[2,80,256]{2,1,0:T(8,128)(2,1)S(1)}, bf16[2,80,256]{2,1,0:T(8,128)(2,1)S(1)}, u32[]{:S(2)}, u32[]{:S(2)}) collective-permute-start(bf16[2,80,256]{2,1,0:T(8,128)(2,1)S(1)} %collective-permute-done.18.refs_7_), channel_id=1, source_target_pairs={{0,4},{4,8},{8,12},{12,16},{16,20},{20,24},{24,28},{28,0},{1,5},{5... | collective-permute-start | bytes 245768 | tf_op jit(solution)/shard_map/ppermute | solution.py:22
  25.1 7.5 %collective-permute-start.16 = (bf16[2,80,256]{2,1,0:T(8,128)(2,1)S(1)}, bf16[2,80,256]{2,1,0:T(8,128)(2,1)S(1)}, u32[]{:S(2)}, u32[]{:S(2)}) collective-permute-start(bf16[2,80,256]{2,1,0:T(8,128)(2,1)S(1)} %collective-permute-done.15.refs_2_), channel_id=1, source_target_pairs={{0,28},{4,0},{8,4},{12,8},{16,12},{20,16},{24,20},{28,24},{1,29},{... | collective-permute-start | bytes 245768 | tf_op jit(solution)/shard_map/ppermute | solution.py:22
  28.7 13.5 %collective-permute-start.3 = (bf16[2,80,256]{2,1,0:T(8,128)(2,1)S(1)}, bf16[2,80,256]{2,1,0:T(8,128)(2,1)S(1)}, u32[]{:S(2)}, u32[]{:S(2)}) collective-permute-start(bf16[2,80,256]{2,1,0:T(8,128)(2,1)S(1)} %get-tuple-element.17.refs_0_), channel_id=1, source_target_pairs={{0,192},{64,0},{128,64},{192,128},{1,193},{65,1},{129,65},{193,129... | collective-permute-start | bytes 245768 | tf_op jit(solution)/shard_map/ppermute | solution.py:22
  29.4 12.7 %collective-permute-start.4 = (bf16[2,80,256]{2,1,0:T(8,128)(2,1)S(1)}, bf16[2,80,256]{2,1,0:T(8,128)(2,1)S(1)}, u32[]{:S(2)}, u32[]{:S(2)}) collective-permute-start(bf16[2,80,256]{2,1,0:T(8,128)(2,1)S(1)} %get-tuple-element.17.refs_0_), channel_id=1, source_target_pairs={{0,128},{64,192},{128,0},{192,64},{1,129},{65,193},{129,1},{193,65... | collective-permute-start | bytes 245768 | tf_op jit(solution)/shard_map/ppermute | solution.py:22
  30.4 11.8 %collective-permute-start.5 = (bf16[2,80,256]{2,1,0:T(8,128)(2,1)S(1)}, bf16[2,80,256]{2,1,0:T(8,128)(2,1)S(1)}, u32[]{:S(2)}, u32[]{:S(2)}) collective-permute-start(bf16[2,80,256]{2,1,0:T(8,128)(2,1)S(1)} %get-tuple-element.17.refs_0_), channel_id=1, source_target_pairs={{0,64},{64,128},{128,192},{192,0},{1,65},{65,129},{129,193},{193,1... | collective-permute-start | bytes 245768 | tf_op jit(solution)/shard_map/ppermute | solution.py:22
  32.5 12.4 %collective-permute-start.20 = (bf16[2,80,256]{2,1,0:T(8,128)(2,1)S(1)}, bf16[2,80,256]{2,1,0:T(8,128)(2,1)S(1)}, u32[]{:S(2)}, u32[]{:S(2)}) collective-permute-start(bf16[2,80,256]{2,1,0:T(8,128)(2,1)S(1)} %collective-permute-done.19.refs_6_), channel_id=1, source_target_pairs={{0,4},{4,8},{8,12},{12,16},{16,20},{20,24},{24,28},{28,0},{1,5},{5... | collective-permute-start | bytes 245768 | tf_op jit(solution)/shard_map/ppermute | solution.py:22
  32.5 12.4 %collective-permute-start.17 = (bf16[2,80,256]{2,1,0:T(8,128)(2,1)S(1)}, bf16[2,80,256]{2,1,0:T(8,128)(2,1)S(1)}, u32[]{:S(2)}, u32[]{:S(2)}) collective-permute-start(bf16[2,80,256]{2,1,0:T(8,128)(2,1)S(1)} %collective-permute-done.16.refs_3_), channel_id=1, source_target_pairs={{0,28},{4,0},{8,4},{12,8},{16,12},{20,16},{24,20},{28,24},{1,29},{... | collective-permute-start | bytes 245768 | tf_op jit(solution)/shard_map/ppermute | solution.py:22
  35.8 1.7 %copy-start = (bf16[1280,1024]{1,0:T(8,128)(2,1)S(1)}, bf16[1280,1024]{1,0:T(8,128)(2,1)}, u32[]{:S(2)}) copy-start(bf16[1280,1024]{1,0:T(8,128)(2,1)} %w.6) | copy-start | bytes 7864324
  37.5 17.9 %copy-start.1 = (bf16[1280,1024]{1,0:T(8,128)(2,1)S(1)}, bf16[1280,1024]{1,0:T(8,128)(2,1)}, u32[]{:S(2)}) copy-start(bf16[1280,1024]{1,0:T(8,128)(2,1)} %w.6) | copy-start | bytes 7864324
  42.1 19.0 %collective-permute-start.1 = (bf16[1536,256]{1,0:T(8,128)(2,1)}, bf16[1536,256]{1,0:T(8,128)(2,1)}, u32[]{:S(2)}, u32[]{:S(2)}) collective-permute-start(bf16[1536,256]{1,0:T(8,128)(2,1)} %shard_map.77), channel_id=1, source_target_pairs={{0,1},{1,0},{2,3},{3,2},{4,5},{5,4},{6,7},{7,6},{8,9},{9,8},{10,11... | collective-permute-start | bytes 2359304 | tf_op jit(solution)/shard_map/ppermute | solution.py:22
  42.9 10.4 %collective-permute-start.6 = (bf16[4,2,80,256]{3,2,1,0:T(8,128)(2,1)}, bf16[4,2,80,256]{3,2,1,0:T(8,128)(2,1)}, u32[]{:S(2)}, u32[]{:S(2)}) collective-permute-start(bf16[4,2,80,256]{3,2,1,0:T(8,128)(2,1)} %shard_map.82.refs_0_), channel_id=1, source_target_pairs={{0,28},{4,0},{8,4},{12,8},{16,12},{20,16},{24,20},{28,24},{1,29},{... | collective-permute-start | bytes 983048 | tf_op jit(solution)/shard_map/ppermute | solution.py:22
  42.9 11.9 %collective-permute-start.7 = (bf16[4,2,80,256]{3,2,1,0:T(8,128)(2,1)}, bf16[4,2,80,256]{3,2,1,0:T(8,128)(2,1)}, u32[]{:S(2)}, u32[]{:S(2)}) collective-permute-start(bf16[4,2,80,256]{3,2,1,0:T(8,128)(2,1)} %shard_map.82.refs_0_), channel_id=1, source_target_pairs={{0,4},{4,8},{8,12},{12,16},{16,20},{20,24},{24,28},{28,0},{1,5},{5... | collective-permute-start | bytes 983048 | tf_op jit(solution)/shard_map/ppermute | solution.py:22
  45.9 24.7 %collective-permute-start.21 = (bf16[2,640,256]{2,1,0:T(8,128)(2,1)}, bf16[2,640,256]{2,1,0:T(8,128)(2,1)}, u32[]{:S(2)}, u32[]{:S(2)}) collective-permute-start(bf16[2,640,256]{2,1,0:T(8,128)(2,1)} %shard_map.83.refs_0_), channel_id=1, source_target_pairs={{0,192},{64,0},{128,64},{192,128},{1,193},{65,1},{129,65},{193,129... | collective-permute-start | bytes 1966088 | tf_op jit(solution)/shard_map/ppermute | solution.py:22
  46.1 25.5 %collective-permute-start.23 = (bf16[2,640,256]{2,1,0:T(8,128)(2,1)}, bf16[2,640,256]{2,1,0:T(8,128)(2,1)}, u32[]{:S(2)}, u32[]{:S(2)}) collective-permute-start(bf16[2,640,256]{2,1,0:T(8,128)(2,1)} %shard_map.83.refs_0_), channel_id=1, source_target_pairs={{0,64},{64,128},{128,192},{192,0},{1,65},{65,129},{129,193},{193,1... | collective-permute-start | bytes 1966088 | tf_op jit(solution)/shard_map/ppermute | solution.py:22
  53.3 13.0 %collective-permute-start.8 = (bf16[4,2,80,256]{3,2,1,0:T(8,128)(2,1)}, bf16[4,2,80,256]{3,2,1,0:T(8,128)(2,1)}, u32[]{:S(2)}, u32[]{:S(2)}) collective-permute-start(bf16[4,2,80,256]{3,2,1,0:T(8,128)(2,1)} %collective-permute-done.6.refs_1_), channel_id=1, source_target_pairs={{0,28},{4,0},{8,4},{12,8},{16,12},{20,16},{24,20},{28,24},{1,29},{... | collective-permute-start | bytes 983048 | tf_op jit(solution)/shard_map/ppermute | solution.py:22
  54.8 13.0 %collective-permute-start.9 = (bf16[4,2,80,256]{3,2,1,0:T(8,128)(2,1)}, bf16[4,2,80,256]{3,2,1,0:T(8,128)(2,1)}, u32[]{:S(2)}, u32[]{:S(2)}) collective-permute-start(bf16[4,2,80,256]{3,2,1,0:T(8,128)(2,1)} %collective-permute-done.7.refs_2_), channel_id=1, source_target_pairs={{0,4},{4,8},{8,12},{12,16},{16,20},{20,24},{24,28},{28,0},{1,5},{5... | collective-permute-start | bytes 983048 | tf_op jit(solution)/shard_map/ppermute | solution.py:22
  61.1 5.2 %copy-start.3 = (f32[1536,256]{1,0:T(8,128)}, f32[1536,256]{1,0:T(8,128)S(1)}, u32[]{:S(2)}) copy-start(f32[1536,256]{1,0:T(8,128)S(1)} %get-tuple-element.15.own) | copy-start | bytes 4718596
  61.1 37.2 %collective-permute-start = (bf16[1536,256]{1,0:T(8,128)(2,1)}, bf16[1536,256]{1,0:T(8,128)(2,1)}, u32[]{:S(2)}, u32[]{:S(2)}) collective-permute-start(bf16[1536,256]{1,0:T(8,128)(2,1)} %get-tuple-element.16), channel_id=1, source_target_pairs={{0,1},{1,0},{2,3},{3,2},{4,5},{5,4},{6,7},{7,6},{8,9},{9,8},{10,11... | collective-permute-start | bytes 2359304 | tf_op jit(solution)/shard_map/ppermute | solution.py:22
  66.3 32.0 %collective-permute-start.2 = (bf16[1536,256]{1,0:T(8,128)(2,1)}, bf16[1536,256]{1,0:T(8,128)(2,1)S(1)}, u32[]{:S(2)}, u32[]{:S(2)}) collective-permute-start(bf16[1536,256]{1,0:T(8,128)(2,1)} %shard_map.78), channel_id=1, source_target_pairs={{0,2},{2,0},{1,3},{3,1},{4,6},{6,4},{5,7},{7,5},{8,10},{10,8},{9,1... | collective-permute-start | bytes 2359304 | tf_op jit(solution)/shard_map/ppermute | solution.py:22
  67.9 9.8 %collective-permute-start.10 = (bf16[4,2,80,256]{3,2,1,0:T(8,128)(2,1)}, bf16[4,2,80,256]{3,2,1,0:T(8,128)(2,1)S(1)}, u32[]{:S(2)}, u32[]{:S(2)}) collective-permute-start(bf16[4,2,80,256]{3,2,1,0:T(8,128)(2,1)} %collective-permute-done.8.refs_3_), channel_id=1, source_target_pairs={{0,28},{4,0},{8,4},{12,8},{16,12},{20,16},{24,20},{28,24},{1,29},{... | collective-permute-start | bytes 983048 | tf_op jit(solution)/shard_map/ppermute | solution.py:22
  70.6 10.4 %collective-permute-start.11 = (bf16[4,2,80,256]{3,2,1,0:T(8,128)(2,1)}, bf16[4,2,80,256]{3,2,1,0:T(8,128)(2,1)S(1)}, u32[]{:S(2)}, u32[]{:S(2)}) collective-permute-start(bf16[4,2,80,256]{3,2,1,0:T(8,128)(2,1)} %collective-permute-done.9.refs_4_), channel_id=1, source_target_pairs={{0,4},{4,8},{8,12},{12,16},{16,20},{20,24},{24,28},{28,0},{1,5},{5... | collective-permute-start | bytes 983048 | tf_op jit(solution)/shard_map/ppermute | solution.py:22
  71.6 11.5 %collective-permute-start.22 = (bf16[640,256]{1,0:T(8,128)(2,1)S(1)}, bf16[640,256]{1,0:T(8,128)(2,1)S(1)}, u32[]{:S(2)}, u32[]{:S(2)}) collective-permute-start(bf16[640,256]{1,0:T(8,128)(2,1)S(1)} %slice_bitcast_fusion.1), channel_id=1, source_target_pairs={{0,192},{64,0},{128,64},{192,128},{1,193},{65,1},{129,65},{193,129... | collective-permute-start | bytes 983048 | tf_op jit(solution)/shard_map/ppermute | solution.py:22
  77.7 13.3 %collective-permute-start.24 = (bf16[640,256]{1,0:T(8,128)(2,1)}, bf16[640,256]{1,0:T(8,128)(2,1)S(1)}, u32[]{:S(2)}, u32[]{:S(2)}) collective-permute-start(bf16[640,256]{1,0:T(8,128)(2,1)} %slice_bitcast_fusion), channel_id=1, source_target_pairs={{0,64},{64,128},{128,192},{192,0},{1,65},{65,129},{129,193},{193,1... | collective-permute-start | bytes 983048 | tf_op jit(solution)/shard_map/ppermute | solution.py:22
  81.0 11.8 %collective-permute-start.12 = (bf16[2,2,80,256]{3,2,1,0:T(8,128)(2,1)S(1)}, bf16[2,2,80,256]{3,2,1,0:T(8,128)(2,1)S(1)}, u32[]{:S(2)}, u32[]{:S(2)}) collective-permute-start(bf16[2,2,80,256]{3,2,1,0:T(8,128)(2,1)S(1)} %slice.16), channel_id=1, source_target_pairs={{0,28},{4,0},{8,4},{12,8},{16,12},{20,16},{24,20},{28,24},{1,29},{... | collective-permute-start | bytes 491528 | tf_op jit(solution)/shard_map/ppermute | solution.py:22
  83.1 9.7 %collective-permute-start.13 = (bf16[2,2,80,256]{3,2,1,0:T(8,128)(2,1)}, bf16[2,2,80,256]{3,2,1,0:T(8,128)(2,1)S(1)}, u32[]{:S(2)}, u32[]{:S(2)}) collective-permute-start(bf16[2,2,80,256]{3,2,1,0:T(8,128)(2,1)} %slice.17), channel_id=1, source_target_pairs={{0,4},{4,8},{8,12},{12,16},{16,20},{20,24},{24,28},{28,0},{1,5},{5... | collective-permute-start | bytes 491528 | tf_op jit(solution)/shard_map/ppermute | solution.py:22
  92.8 5.6 %copy-start.2 = (f32[1536,128]{1,0:T(8,128)S(1)}, f32[1536,128]{1,0:T(8,128)}, u32[]{:S(2)}) copy-start(f32[1536,128]{1,0:T(8,128)} %get-tuple-element.28.cosine) | copy-start | bytes 2359300
  92.8 5.6 %copy-start.4 = (f32[1536,256]{1,0:T(8,128)S(1)}, f32[1536,256]{1,0:T(8,128)}, u32[]{:S(2)}) copy-start(f32[1536,256]{1,0:T(8,128)} %copy-done.3) | copy-start | bytes 4718596
  92.8 5.6 %copy-start.5 = (f32[128]{0:T(128)S(1)}, f32[128]{0:T(128)}, u32[]{:S(2)}) copy-start(f32[128]{0:T(128)} %param.7) | copy-start | bytes 1540
